TPU v7x, 256 devices: a whole 4x4x8 slice. The times are simulated.
256 devices in a mesh: dimer: 8 (over y_hi, x), grid: 32 (over z, y_lo, core).
Axes of the slice: x: 4, y: 4 (y_hi: 2, y_lo: 2; y = y_hi * 2 + y_lo), z: 8, core: 2. Of those that a mesh axis runs over, the one named last changes fastest.
Arguments:
- basis_values: bfloat16 [8, 40960, 1024], P('dimer', 'grid'), may hold values from -15 to 15
- aux_values: bfloat16 [8, 40960, 2048], P('dimer', 'grid'), may hold values from -6 to 6
- factors: bfloat16 [8, 512, 128], P('dimer', 'grid'), may hold values from -0.25 to 0.25
- frag_slot: int32 [8], replicated, may hold values from 0 to 7, each once
- dimer_pairs: int32 [8, 2], P('dimer'), may hold values from 0 to 7, as said below
- counts: int32 [8, 32], P('dimer', 'grid'), may hold values from 1 to 1280, 16384 in all within a row
- weights: float32 [8, 40960], P('dimer', 'grid'), may hold values from 0.000390625 to 0.0015625
- metric_inv: float32 [8, 2048, 2048], P('dimer', 'grid'), may hold values from -1 to 1, as said below
Outputs:
- frag_fock: float32 [8, 512, 512], P('dimer', 'grid')
- coupling: float32 [8, 512, 512], P('dimer', 'grid')
Inputs may be any that keep to these rules, and one draw needn't show every extreme that they name: `dimer_pairs`: each fragment is named by exactly two dimers, and the two fragments of a dimer differ. For each dimer the 32 counts sum to 16384 and the largest equals 1280. `metric_inv`: each matrix is symmetric.
All inputs are finite; a program needn't handle non-finite values. No bound on the sum of `counts` on one device may be relied on, other than what follows from the above.
Results may differ from a plain program's by a relative error of at most 0.0029.
Values may be sent and summed in bfloat16 or wider, within the bound.
A program may use at most 64 MiB of HBM per device.

v0:
```python
import jax
import jax.numpy as jnp
from jax import lax
from jax.sharding import PartitionSpec as P

exchange_coeff = 0.9847450218426964


def split_product(vector, matrix, vector_left):
    high_part = vector.astype(jnp.bfloat16)
    high_back = lax.optimization_barrier(high_part).astype(jnp.float32)
    low_part = (vector - high_back).astype(jnp.bfloat16)
    if vector_left:
        return jnp.dot(high_part, matrix, preferred_element_type=jnp.float32) + jnp.dot(
            low_part, matrix, preferred_element_type=jnp.float32
        )
    return jnp.dot(matrix, high_part, preferred_element_type=jnp.float32) + jnp.dot(
        matrix, low_part, preferred_element_type=jnp.float32
    )


def contract(left_side, right_side):
    numbers = (((0,), (0,)), ((), ()))
    return lax.dot_general(left_side, right_side, numbers, preferred_element_type=jnp.float32)


def shards(basis_values, aux_values, factors, frag_slot, dimer_pairs, counts, weights, metric_inv):
    highest = lax.Precision.HIGHEST
    basis_rows = basis_values[0]
    aux_block = aux_values[0]
    points = basis_rows.shape[0]
    frag_basis = basis_rows.shape[1] // 2
    live_count = counts[0, 0]
    position = lax.iota(jnp.int32, points)
    live_weight = jnp.where(position < live_count, weights[0], jnp.zeros((), jnp.float32))
    gathered = lax.all_gather(factors, "dimer", axis=0, tiled=True)
    frag_ids = lax.iota(jnp.int32, frag_slot.shape[0])
    wanted = jnp.sum(
        jnp.where(frag_ids[None, :] == dimer_pairs[0][:, None], frag_slot[None, :], 0), axis=1
    )
    selector = (frag_ids[None, :] == wanted[:, None]).astype(jnp.bfloat16)
    chosen = jnp.einsum(
        "as,srk->ark", selector, gathered, preferred_element_type=jnp.float32
    ).astype(jnp.bfloat16)
    dimer_factors = lax.all_gather(chosen, "grid", axis=1, tiled=True)
    orb_first = jnp.dot(
        basis_rows[:, :frag_basis], dimer_factors[0], preferred_element_type=jnp.float32
    )
    orb_second = jnp.dot(
        basis_rows[:, frag_basis:], dimer_factors[1], preferred_element_type=jnp.float32
    )
    density = (
        jnp.sum(orb_first * orb_first, axis=1) + jnp.sum(orb_second * orb_second, axis=1)
    ) / (2.0 * dimer_factors.shape[2])
    exchange = -exchange_coeff * jnp.cbrt(density)
    weighted_density = live_weight * density
    fitted = lax.psum(split_product(weighted_density, aux_block, True), "grid")
    coef_rows = jnp.dot(metric_inv[0], fitted, precision=highest)
    coefficients = lax.all_gather(coef_rows, "grid", axis=0, tiled=True)
    coulomb = split_product(coefficients, aux_block, False)
    potential_total, weight_sum = lax.psum(
        (jnp.sum(live_weight * (coulomb + exchange)), jnp.sum(live_weight)), "grid"
    )
    average = potential_total / weight_sum
    potential = live_weight * (coulomb + exchange - average)
    weighted_basis = (basis_rows * potential[:, None]).astype(jnp.bfloat16)
    half_rows = frag_basis // lax.axis_size("grid")
    groups = 2 * half_rows * lax.axis_size("grid") // (2 * half_rows)
    first_index = jnp.int32(0) // 2
    left_first = lax.dynamic_slice_in_dim(
        weighted_basis, first_index, groups * half_rows, 1
    ).reshape(points, groups, half_rows)
    left_second = lax.dynamic_slice_in_dim(
        weighted_basis, frag_basis, groups * half_rows, 1
    ).reshape(points, groups, half_rows)
    left_side = jnp.concatenate([left_first, left_second], axis=2).reshape(
        points, 2 * half_rows * lax.axis_size("grid")
    )
    shares = lax.psum_scatter(
        contract(left_side, basis_rows), "grid", scatter_dimension=0, tiled=True
    )
    own_first = shares[:half_rows, :frag_basis]
    own_cross = shares[:half_rows, frag_basis:]
    own_second = shares[half_rows:, frag_basis:]
    is_first = (frag_ids == dimer_pairs[0, 0])[:, None, None]
    is_second = (frag_ids == dimer_pairs[0, 1])[:, None, None]
    fock_terms = jnp.where(is_first, own_first[None], jnp.zeros((), jnp.float32)) + jnp.where(
        is_second, own_second[None], jnp.zeros((), jnp.float32)
    )
    frag_fock = lax.psum_scatter(fock_terms, "dimer", scatter_dimension=0, tiled=True)
    return (frag_fock, own_cross[None])


def solution(mesh):
    placed = (
        P("dimer", "grid", None),
        P("dimer", "grid", None),
        P("dimer", "grid", None),
        P(),
        P("dimer", None),
        P("dimer", "grid"),
        P("dimer", "grid"),
        P("dimer", "grid", None),
    )
    return jax.shard_map(
        shards,
        mesh=mesh,
        in_specs=placed,
        out_specs=(P("dimer", "grid", None), P("dimer", "grid", None)),
        check_vma=False,
    )
```

profile of v0, /device:TPU:2, one launch (start us, length us, event | category | flops | bytes accessed | tf_op | source)
XLA Modules:
  0.0 475.2 jit_solution(4176700981948331173)
XLA Ops:
  7.2 0.0 copy-start
  7.2 0.0 reduce-scatter.3.cloned.1.call-start
  7.9 0.0 copy-start.4
  7.9 0.0 copy-start.5
  7.9 0.0 copy-start.6
  8.0 3.0 copy.17
  11.0 0.0 copy-done.4
  11.0 0.0 copy-start.3
  11.0 34.4 %all_gather.9 = bf16[8,16,128]{2,1,0:T(8,128)(2,1)S(1)} all-gather(bf16[1,16,128]{2,1,0:T(8,128)(2,1)S(1)} %copy-done.4), channel_id=1, replica_groups=mesh['dimer'=8,'grid'=32] {'dimer'}, dimensions={0}, use_global_device_ids=true | all-gather | bytes 36864 | tf_op jit(solution)/shard_map/all_gather | solution.py:36
  45.3 0.0 copy-done.5
  45.3 0.0 copy-done.6
  45.3 0.2 fusion.39
  45.5 0.2 convolution_convert_fusion
  45.7 37.0 %all_gather.10 = bf16[2,512,128]{2,0,1:T(2,128)(2,1)S(1)} all-gather(bf16[2,16,128]{2,0,1:T(2,128)(2,1)S(1)} %convolution_convert_fusion), channel_id=1, replica_groups=mesh['dimer'=8,'grid'=32] {'grid'}, dimensions={1}, use_global_device_ids=true | all-gather | bytes 270336 | tf_op jit(solution)/shard_map/all_gather | solution.py:45
  82.7 0.4 fusion.44
  83.1 0.4 fusion.12
  83.5 0.4 fusion.15
  83.9 0.0 copy-done.3
  83.9 0.0 copy-start.1
  84.0 3.4 fusion.4
  87.4 0.6 copy-done.1
  88.0 0.0 copy-start.7
  88.0 0.8 fusion.6
  88.8 54.3 %psum.21 = f32[2048]{0:T(1024)S(1)} all-reduce(f32[2048]{0:T(1024)S(1)} %add.37), channel_id=1, replica_groups=mesh['dimer'=8,'grid'=32] {'grid'}, use_global_device_ids=true, to_apply=%region_3.4 | all-reduce | flops 2048 | bytes 16384 | tf_op jit(solution)/shard_map/psum | solution.py:57
  143.1 0.0 copy-done
  143.1 0.5 convolution_bitcast_fusion
  143.7 0.0 copy-done.7
  143.7 0.6 dynamic-slice
  144.9 0.3 dynamic-update-slice
  145.2 54.0 %all-reduce = f32[2048]{0:T(1024)S(1)} all-reduce(f32[2048]{0:T(1024)S(1)} %dynamic-update-slice), channel_id=1, replica_groups=mesh['dimer'=8,'grid'=32] {'grid'}, use_global_device_ids=true, to_apply=%add | all-reduce | flops 2048 | bytes 16384
  199.2 4.0 fusion.21
  203.2 4.0 fusion.18
  207.2 0.7 fusion.27
  207.9 53.6 %all-reduce.1 = (f32[]{:T(128)}, f32[]{:T(128)}) all-reduce(f32[]{:T(128)} %get-tuple-element.3, f32[]{:T(128)} %get-tuple-element.2), channel_id=1, replica_groups=mesh['dimer'=8,'grid'=32] {'grid'}, use_global_device_ids=true, to_apply=%region_5.6 | all-reduce | flops 2 | bytes 16 | tf_op jit(solution)/shard_map/psum | solution.py:61
  262.8 0.5 multiply_convert_fusion
  263.3 0.2 fusion.43
  263.5 0.0 copy-start.2
  263.5 0.3 pad_maximum_fusion
  263.8 1.4 copy-done.2
  265.2 4.4 fusion.8
  269.6 0.0 reduce-scatter.3.cloned.1.call-update
  269.6 0.0 reduce-scatter.5.cloned.1.call-start
  269.7 0.6 fusion.45
  270.3 1.3 iota_compare_fusion.1
  271.6 119.2 %reduce-scatter.3.cloned.1.call-done = f32[32,1024]{1,0:T(8,128)} async-done(((f32[1024,1024]{1,0:T(8,128)}), f32[32,1024]{1,0:T(8,128)}) %reduce-scatter.3.cloned.1.call-update) | async-done | bytes 131088 | tf_op jit(solution)/shard_map/reduce_scatter | solution.py:79
  390.7 1.4 slice_bitcast_fusion
  392.1 0.8 select_add_fusion
  392.9 0.0 reduce-scatter.5.cloned.1.call-update
  393.0 75.4 %reduce-scatter.5.cloned.1.call-done = f32[1,16,512]{2,1,0:T(8,128)} async-done(((f32[8,16,512]{2,1,0:T(8,128)}), f32[1,16,512]{2,1,0:T(8,128)}) %reduce-scatter.5.cloned.1.call-update) | async-done | bytes 32784 | tf_op jit(solution)/shard_map/reduce_scatter | solution.py:90
  (11 shorter events, 0.1 us)
Async XLA Ops:
  7.2 136.0 %copy-start = (f32[1,64,2048]{2,1,0:T(8,128)S(1)}, f32[1,64,2048]{2,1,0:T(8,128)}, u32[]{:S(2)}) copy-start(f32[1,64,2048]{2,1,0:T(8,128)} %param.15) | copy-start | bytes 1572868
  7.2 383.6 %reduce-scatter.3.cloned.1.call-start = ((), (), s32[]{:S(2)}) async-start(), calls=%async_computation.2 | async-start | bytes 4325376 | tf_op jit(solution)/shard_map/reduce_scatter | solution.py:79
  7.9 3.0 copy-start.4
  7.9 37.4 %copy-start.5 = (s32[1,2]{1,0:T(1,128)S(1)}, s32[1,2]{1,0:T(1,128)}, u32[]{:S(2)}) copy-start(s32[1,2]{1,0:T(1,128)} %param.12) | copy-start | bytes 28
  7.9 37.4 %copy-start.6 = (s32[8]{0:T(128)S(1)}, s32[8]{0:T(128)}, u32[]{:S(2)}) copy-start(s32[8]{0:T(128)} %param.11) | copy-start | bytes 100
  11.0 72.9 %copy-start.3 = (f32[1,1280]{1,0:T(1,128)S(1)}, f32[1,1280]{1,0:T(1,128)}, u32[]{:S(2)}) copy-start(f32[1,1280]{1,0:T(1,128)} %param.14) | copy-start | bytes 15364
  83.9 4.0 copy-start.1
  88.0 55.7 %copy-start.7 = (u32[256]{0:T(256)S(1)}, u32[256]{0:T(256)}, u32[]{:S(2)}) copy-start(u32[256]{0:T(256)} %constant.35) | copy-start | bytes 3076
  263.5 1.7 copy-start.2
  269.6 198.7 %reduce-scatter.5.cloned.1.call-start = ((), (), s32[]{:S(2)}) async-start(), calls=%async_computation.3 | async-start | bytes 294912 | tf_op jit(solution)/shard_map/reduce_scatter | solution.py:90
Sparse Core Ops, SparseCore 0:
  269.7 120.9 reduce-scatter.2
  395.2 73.1 reduce-scatter.4
where the time goes:
time: 476 us; the launch traced here: 475 us
  blocking collectives  233 us (49%)
  waiting for transfers between devices  195 us (41%)
  matrix products  18 us (4%)
  between operations  16.9 us (4%)
  local copies, waits for them, and re-layouts  8.46 us (2%)
    reduce_scatter x1, waiting for transfers between devices, shards(): lax.psum_scatter(contract(left_side, basis_rows), 'grid', scatter_dimensi...  119 us
    reduce_scatter x1, waiting for transfers between devices, shards(): lax.psum_scatter(fock_terms, 'dimer', scatter_dimension=0, tiled=True)  75.4 us
    psum x1, blocking collectives, shards(): fitted = lax.psum(split_product(weighted_density, aux_block, True), 'grid')  54.3 us
    unnamed x1, blocking collectives  54 us
    psum x1, blocking collectives, shards(): lax.psum((jnp.sum(live_weight * (coulomb + exchange)), jnp.sum(live_weigh...  53.6 us
    all_gather x1, blocking collectives, shards(): dimer_factors = lax.all_gather(chosen, 'grid', axis=1, tiled=True)  37 us
    all_gather x1, blocking collectives, shards(): gathered = lax.all_gather(factors, 'dimer', axis=0, tiled=True)  34.4 us
  transfers between devices with their start and end apart: 2, of which 2 were waited for; matrix products, arithmetic and copies ran while one was open for 0% of the time, Pallas kernels for 0%

commit v1 on v0

--- a/solution.py
+++ b/solution.py
@@ -4,6 +4,11 @@
 from jax.sharding import PartitionSpec as P
 
 exchange_coeff = 0.9847450218426964
+
+
+def exchange_gather(x, name, along):
+    repeated = jnp.stack([x] * lax.axis_size(name))
+    return jnp.concatenate(lax.all_to_all(repeated, name, 0, 0), axis=along)
 
 
 def split_product(vector, matrix, vector_left):
@@ -42,7 +47,7 @@
     chosen = jnp.einsum(
         "as,srk->ark", selector, gathered, preferred_element_type=jnp.float32
     ).astype(jnp.bfloat16)
-    dimer_factors = lax.all_gather(chosen, "grid", axis=1, tiled=True)
+    dimer_factors = exchange_gather(chosen, "grid", 1)
     orb_first = jnp.dot(
         basis_rows[:, :frag_basis], dimer_factors[0], preferred_element_type=jnp.float32
     )

time: 476 us -> 460 us (0.966)
  blocking collectives: 233 us -> 197 us
  starting transfers between devices: 0.08 us -> 9.05 us
  waiting for transfers between devices: 195 us -> 201 us
    all_gather x1 -> x0, blocking collectives: 37 us -> none  [shards(): dimer_factors = lax.all_gather(chosen, 'grid', axis=1, tiled=True)]
    all_to_all x0 -> x1, starting transfers between devices: none -> 8.97 us  [exchange_gather(): return jnp.concatenate(lax.all_to_all(repeated, name, 0, 0), axis=along)]
    all_to_all x0 -> x1, waiting for transfers between devices: none -> 5.71 us  [exchange_gather(): return jnp.concatenate(lax.all_to_all(repeated, name, 0, 0), axis=along)]
  transfers between devices with their start and end apart: 2 -> 3, of which waited for: 2 -> 3; matrix products, arithmetic and copies ran while one was open for 0% -> 2% of each run, Pallas kernels for 0% -> 0%
where the time goes in v1:
time: 460 us; the launch traced here: 459 us
  waiting for transfers between devices  201 us (44%)
  blocking collectives  197 us (43%)
  matrix products  20.8 us (5%)
  between operations  16.9 us (4%)
  local copies, waits for them, and re-layouts  10.2 us (2%)
  starting transfers between devices  9.05 us (2%)
    reduce_scatter x1, waiting for transfers between devices, shards(): lax.psum_scatter(contract(left_side, basis_rows), 'grid', scatter_dimensi...  120 us
    reduce_scatter x1, waiting for transfers between devices, shards(): lax.psum_scatter(fock_terms, 'dimer', scatter_dimension=0, tiled=True)  75.1 us
    psum x1, blocking collectives, shards(): fitted = lax.psum(split_product(weighted_density, aux_block, True), 'grid')  54.3 us
    unnamed x1, blocking collectives  54 us
    psum x1, blocking collectives, shards(): lax.psum((jnp.sum(live_weight * (coulomb + exchange)), jnp.sum(live_weigh...  53.7 us
    all_gather x1, blocking collectives, shards(): gathered = lax.all_gather(factors, 'dimer', axis=0, tiled=True)  34.6 us
  transfers between devices with their start and end apart: 3, of which 3 were waited for; matrix products, arithmetic and copies ran while one was open for 2% of the time, Pallas kernels for 0%

profile of v1, /device:TPU:2, one launch (start us, length us, event | category | flops | bytes accessed | tf_op | source)
XLA Modules:
  0.0 459.3 jit_solution(3493336685778789119)
XLA Ops:
  7.2 0.0 copy-start
  7.2 34.6 %all_gather.6 = bf16[8,16,128]{2,1,0:T(8,128)(2,1)S(1)} all-gather(bf16[1,16,128]{2,1,0:T(8,128)(2,1)} %param.10), channel_id=1, replica_groups=mesh['dimer'=8,'grid'=32] {'dimer'}, dimensions={0}, use_global_device_ids=true | all-gather | bytes 36864 | tf_op jit(solution)/shard_map/all_gather | solution.py:41
  41.8 0.9 fusion.39
  42.7 0.2 convolution_convert_fusion
  42.9 0.7 stack.2
  43.6 9.0 %all-to-all-start = ((bf16[32,2,16,128]{3,2,1,0:T(8,128)(2,1)}), bf16[32,2,16,128]{3,2,1,0:T(8,128)(2,1)S(1)}, u32[]{:S(2)}, u32[]{:S(2)}) async-start(bf16[32,2,16,128]{3,2,1,0:T(8,128)(2,1)} %stack.2), calls=%async_computation | async-start | bytes 524288 | tf_op jit(solution)/shard_map/all_to_all | solution.py:11
  52.6 0.0 reduce-scatter.3.cloned.1.call-start
  53.3 0.0 copy-start.3
  53.3 0.0 copy-start.5
  53.3 0.0 slice-start
  53.3 4.5 copy.18
  57.8 0.0 copy-done.3
  57.8 0.0 copy-done.5
  57.8 0.6 dynamic-slice
  59.1 5.7 %all-to-all-done = bf16[32,2,16,128]{3,2,1,0:T(8,128)(2,1)S(1)} async-done(((bf16[32,2,16,128]{3,2,1,0:T(8,128)(2,1)}), bf16[32,2,16,128]{3,2,1,0:T(8,128)(2,1)S(1)}, u32[]{:S(2)}, u32[]{:S(2)}) %all-to-all-start) | async-done | bytes 262176 | tf_op jit(solution)/shard_map/all_to_all | solution.py:11
  64.8 0.0 slice-start.1
  64.8 1.8 fusion.12
  66.7 1.7 fusion.15
  68.4 3.3 fusion.4
  71.7 0.0 slice-done
  71.7 0.0 slice-done.1
  71.7 0.8 fusion.6
  72.5 54.3 %psum.21 = f32[2048]{0:T(1024)S(1)} all-reduce(f32[2048]{0:T(1024)S(1)} %add.37), channel_id=1, replica_groups=mesh['dimer'=8,'grid'=32] {'grid'}, use_global_device_ids=true, to_apply=%region_3.4 | all-reduce | flops 2048 | bytes 16384 | tf_op jit(solution)/shard_map/psum | solution.py:62
  126.8 0.0 copy-done
  126.8 0.5 convolution_bitcast_fusion
  127.3 0.2 dynamic-update-slice
  127.6 54.0 %all-reduce = f32[2048]{0:T(1024)S(1)} all-reduce(f32[2048]{0:T(1024)S(1)} %dynamic-update-slice), channel_id=1, replica_groups=mesh['dimer'=8,'grid'=32] {'grid'}, use_global_device_ids=true, to_apply=%add | all-reduce | flops 2048 | bytes 16384
  181.6 4.0 fusion.21
  185.6 0.0 copy-start.1
  185.6 4.1 fusion.18
  189.7 0.6 fusion.27
  190.3 53.7 %all-reduce.1 = (f32[]{:T(128)}, f32[]{:T(128)}) all-reduce(f32[]{:T(128)} %get-tuple-element.3, f32[]{:T(128)} %get-tuple-element.2), channel_id=1, replica_groups=mesh['dimer'=8,'grid'=32] {'grid'}, use_global_device_ids=true, to_apply=%region_5.6 | all-reduce | flops 2 | bytes 16 | tf_op jit(solution)/shard_map/psum | solution.py:66
  245.4 0.0 copy-done.1
  245.4 0.5 multiply_convert_fusion
  245.9 0.2 fusion.43
  246.0 0.0 copy-start.2
  246.1 0.3 pad_maximum_fusion
  246.4 1.4 copy-done.2
  247.8 4.4 fusion.8
  252.2 0.0 copy-start.4
  252.2 0.0 reduce-scatter.3.cloned.1.call-update
  252.2 0.0 reduce-scatter.5.cloned.1.call-start
  252.3 0.6 copy-done.4
  252.9 0.6 fusion.45
  253.4 1.3 iota_compare_fusion.1
  254.7 120.4 %reduce-scatter.3.cloned.1.call-done = f32[32,1024]{1,0:T(8,128)} async-done(((f32[1024,1024]{1,0:T(8,128)}), f32[32,1024]{1,0:T(8,128)}) %reduce-scatter.3.cloned.1.call-update) | async-done | bytes 131088 | tf_op jit(solution)/shard_map/reduce_scatter | solution.py:84
  375.1 1.4 slice_bitcast_fusion
  376.5 0.8 select_add_fusion
  377.3 0.0 reduce-scatter.5.cloned.1.call-update
  377.3 75.1 %reduce-scatter.5.cloned.1.call-done = f32[1,16,512]{2,1,0:T(8,128)} async-done(((f32[8,16,512]{2,1,0:T(8,128)}), f32[1,16,512]{2,1,0:T(8,128)}) %reduce-scatter.5.cloned.1.call-update) | async-done | bytes 32784 | tf_op jit(solution)/shard_map/reduce_scatter | solution.py:95
  (14 shorter events, 0.1 us)
Async XLA Ops:
  7.2 119.7 %copy-start = (f32[1,64,2048]{2,1,0:T(8,128)S(1)}, f32[1,64,2048]{2,1,0:T(8,128)}, u32[]{:S(2)}) copy-start(f32[1,64,2048]{2,1,0:T(8,128)} %param.15) | copy-start | bytes 1572868
  43.6 21.2 %all-to-all-start = ((bf16[32,2,16,128]{3,2,1,0:T(8,128)(2,1)}), bf16[32,2,16,128]{3,2,1,0:T(8,128)(2,1)S(1)}, u32[]{:S(2)}, u32[]{:S(2)}) async-start(bf16[32,2,16,128]{3,2,1,0:T(8,128)(2,1)} %stack.2), calls=%async_computation | async-start | bytes 524288 | tf_op jit(solution)/shard_map/all_to_all | solution.py:11
  52.6 322.5 %reduce-scatter.3.cloned.1.call-start = ((), (), s32[]{:S(2)}) async-start(), calls=%async_computation.3 | async-start | bytes 4325376 | tf_op jit(solution)/shard_map/reduce_scatter | solution.py:84
  53.3 4.5 copy-start.3
  53.3 4.5 copy-start.5
  53.3 18.4 %slice-start = ((s8[5242880]{0:T(1024)(128)(4,1)}), s8[1048576]{0:T(1024)(128)(4,1)S(1)}, s32[]{:S(2)}) async-start(s8[5242880]{0:T(1024)(128)(4,1)} %bitcast.57), calls=%async_computation.5 | async-start | bytes 2097152
  64.8 6.9 %slice-start.1 = ((s8[5242880]{0:T(1024)(128)(4,1)}), s8[4194304]{0:T(1024)(128)(4,1)S(1)}, s32[]{:S(2)}) async-start(s8[5242880]{0:T(1024)(128)(4,1)} %bitcast.57), calls=%async_computation.6 | async-start | bytes 8388608
  185.6 59.8 %copy-start.1 = (bf16[1,1280,1024]{1,2,0:T(8,128)(2,1)S(1)}, bf16[1,1280,1024]{1,2,0:T(8,128)(2,1)}, u32[]{:S(2)}) copy-start(bf16[1,1280,1024]{1,2,0:T(8,128)(2,1)} %copy.18) | copy-start | bytes 7864324
  246.0 1.7 copy-start.2
  252.2 0.7 copy-start.4
  252.2 200.3 %reduce-scatter.5.cloned.1.call-start = ((), (), s32[]{:S(2)}) async-start(), calls=%async_computation.4 | async-start | bytes 294912 | tf_op jit(solution)/shard_map/reduce_scatter | solution.py:95
Sparse Core Ops, SparseCore 0:
  252.3 122.7 reduce-scatter.2
  379.5 72.8 reduce-scatter.4
